TPU v7x, 256 devices: a whole 4x4x8 slice. The times are simulated.
256 devices in a mesh: section: 8 (over z), shard: 32 (over y, x, core).
Axes of the slice: x: 4, y: 4, z: 8, core: 2. Of those that a mesh axis runs over, the one named last changes fastest.
Arguments:
- tokens: bfloat16 [4, 64, 8192], P(None, 'shard'), may hold values from -6 to 6
- lengths: int32 [4], replicated, may hold values from 1 to 64, 160 in all
- norm_gain: float32 [8, 8192], P('section'), may hold values from 0.25 to 1.75
- gate_tiles: bfloat16 [8, 128, 28, 128, 128], P('section', 'shard'), may hold values from -0.09375 to 0.09375
- up_tiles: bfloat16 [8, 128, 28, 128, 128], P('section', 'shard'), may hold values from -0.09375 to 0.09375
- in_index: int32 [8, 128, 28], P('section', 'shard'), may hold values from -1 to 63, as said below
- down_tiles: bfloat16 [8, 128, 28, 128, 128], P('section', 'shard'), may hold values from -0.0625 to 0.0625
- out_index: int32 [8, 128, 28], P('section', 'shard'), may hold values from -1 to 63, as said below
Outputs:
- hidden_states: bfloat16 [8, 4, 64, 8192], P('section', None, 'shard')
Inputs may be any that keep to these rules, and one draw needn't show every extreme that they name: `in_index`: each list of 28 slots holds distinct block numbers first and -1 in the slots after them; at least 21 slots of every list hold a block number, and in each layer some list holds 28. `out_index`: each list of 28 slots holds distinct block numbers first and -1 in the slots after them; at least 21 slots of every list hold a block number, and in each layer some list holds 28.
All inputs are finite; a program needn't handle non-finite values.
Results may differ from a plain program's by a relative error of at most 0.035.
Values may be sent and summed in bfloat16 or wider, within the bound.
A program may use at most 128 MiB of HBM per device.

v0:
```python
import jax
import jax.numpy as jnp
from jax import lax
from jax.sharding import PartitionSpec as P

norm_eps = 1e-05


def shifted(value, axis, by):
    size = lax.axis_size(axis)
    pairs = [(i, i + by) for i in range(size) if 0 <= i + by < size]
    return lax.ppermute(value, axis, pairs)


def body(tokens, lengths, norm_gain, gate_tiles, up_tiles, in_index, down_tiles, out_index):
    micro_count, own_count, model_width = tokens.shape
    gain_row = norm_gain[0]
    gate_local = gate_tiles[0]
    up_local = up_tiles[0]
    down_local = down_tiles[0]
    in_local = in_index[0]
    out_local = out_index[0]
    block_size = gate_local.shape[-1]
    block_total = model_width // block_size
    local_blocks = gate_local.shape[0]
    section_id = lax.axis_index("section")
    section_total = lax.axis_size("section")
    shard_id = lax.axis_index("shard")
    in_valid = (in_local >= 0).astype(jnp.bfloat16)
    in_clamped = jnp.maximum(in_local, 0)
    onehot = (
        out_local[:, :, None] == jnp.arange(block_total, dtype=jnp.int32)[None, None, :]
    ).astype(jnp.bfloat16)
    dense_down = jnp.einsum(
        "hkb,hkcf->hcbf", onehot, down_local, preferred_element_type=jnp.bfloat16
    )
    dense_down = dense_down.reshape(local_blocks * block_size, model_width)
    pieces = 1
    unit_rows = own_count // pieces
    unit_count = micro_count * pieces
    turn_count = unit_count + section_total - 1

    def expand(rows_piece):
        row_count = rows_piece.shape[0]
        column_blocks = rows_piece.reshape(row_count, block_total, block_size)
        picked = jnp.take(column_blocks, in_clamped, axis=1) * in_valid[None, :, :, None]
        gate_val = jnp.einsum(
            "nhkc,hkcf->nhf", picked, gate_local, preferred_element_type=jnp.float32
        )
        up_val = jnp.einsum("nhkc,hkcf->nhf", picked, up_local, preferred_element_type=jnp.float32)
        return (
            (jax.nn.silu(gate_val) * up_val)
            .astype(jnp.bfloat16)
            .reshape(row_count, local_blocks * block_size)
        )

    def turn_step(turn, state_pair):
        incoming, stored = state_pair
        unit_id = turn - section_id
        active = (unit_id >= 0) & (unit_id < unit_count)
        unit_clamped = jnp.clip(unit_id, 0, unit_count - 1)
        micro_id = unit_clamped // pieces
        offset = unit_clamped % pieces * unit_rows
        own_rows = lax.dynamic_slice(tokens, (micro_id, offset, 0), (1, unit_rows, model_width))[0]
        arrived = jnp.where(section_id == 0, own_rows, incoming)
        widened = arrived.astype(jnp.float32)
        scale_row = lax.rsqrt(jnp.mean(widened * widened, axis=-1, keepdims=True) + norm_eps)
        normed = (widened * scale_row * gain_row[None, :]).astype(jnp.bfloat16)
        hidden = expand(lax.all_gather(normed, "shard", axis=0, tiled=True))
        summed = lax.psum_scatter(
            jnp.dot(hidden, dense_down, preferred_element_type=jnp.float32).astype(jnp.bfloat16),
            "shard",
            scatter_dimension=0,
            tiled=True,
        ).astype(jnp.float32)
        row_ids = shard_id * own_count + offset + jnp.arange(unit_rows, dtype=jnp.int32)
        keep_row = row_ids < lengths[micro_id]
        result_rows = jnp.where(keep_row[:, None], widened + summed, jnp.float32(0.0)).astype(
            jnp.bfloat16
        )
        updated = lax.dynamic_update_slice(stored, result_rows[None], (micro_id, offset, 0))
        stored = jnp.where(active, updated, stored)
        incoming = shifted(result_rows, "section", 1)
        return (incoming, stored)

    initial = (
        jnp.zeros((unit_rows, model_width), jnp.bfloat16),
        jnp.zeros((micro_count, own_count, model_width), jnp.bfloat16),
    )
    _, stored = lax.fori_loop(0, turn_count, turn_step, initial)
    return stored[None]


def solution(mesh):
    placed = (
        P(None, "shard", None),
        P(),
        P("section", None),
        P("section", "shard", None, None, None),
        P("section", "shard", None, None, None),
        P("section", "shard", None),
        P("section", "shard", None, None, None),
        P("section", "shard", None),
    )
    return jax.shard_map(
        body,
        mesh=mesh,
        in_specs=placed,
        out_specs=P("section", None, "shard", None),
        check_vma=False,
    )
```

profile of v0, /device:TPU:225, one launch (start us, length us, event | category | flops | bytes accessed | tf_op | source)
XLA Modules:
  0.0 2095.7 jit_solution(10388522514055579015)
XLA Ops:
  6.5 8.5 fusion.34
  15.0 23.6 %copy.31 = bf16[64,8,64,128]{3,1,2,0:T(8,128)(2,1)} copy(bf16[64,8,64,128]{3,2,1,0:T(8,128)(2,1)} %bitcast.109) | data formatting | bytes 16777216
  38.8 2049.4 %while.17 = (s32[]{:T(128)}, bf16[2,8192]{1,0:T(2,128)(2,1)S(1)}, bf16[4,2,8192]{2,1,0:T(2,128)(2,1)S(1)}, s32[]{:T(128)}, s32[]{:T(128)}, /*index=5*/s32[4]{0:T...) while((s32[]{:T(128)}, bf16[2,8192]{1,0:T(2,128)(2,1)S(1)}, ...), condition=%wide.region_3.4_spmd, body=%wide.region_0.3_spmd.sunk | while | flops 1011779584 | bytes 53420872 | solution.py:90
  41.0 50.1 %all-gather.5.cloned.1.call-done = bf16[32,2,8192]{2,1,0:T(2,128)(2,1)} async-done(((bf16[1,2,8192]{2,1,0:T(2,128)(2,1)}), bf16[32,2,8192]{2,1,0:T(2,128)(2,1)}) %all-gather.5.cloned.1.call-update) | async-done | bytes 1048592 | tf_op jit(solution)/shard_map/while/body/eval_jaxpr/all_gather | solution.py:69
  91.1 1.8 reshape.96
  94.6 3.1 fusion.63
  98.6 6.0 convolution_convert_fusion.2
  106.9 111.5 %all-reduce.5.cloned.1.call-done = bf16[64,8192]{1,0:T(8,128)(2,1)} async-done(((bf16[64,8192]{1,0:T(8,128)(2,1)}), bf16[64,8192]{1,0:T(8,128)(2,1)}) %all-reduce.5.cloned.1.call-update) | async-done | bytes 1048592 | tf_op jit(solution)/shard_map/while
  220.8 3.4 collective-permute-done
  226.0 51.6 %all-gather.5.cloned.1.call-done = bf16[32,2,8192]{2,1,0:T(2,128)(2,1)} async-done(((bf16[1,2,8192]{2,1,0:T(2,128)(2,1)}), bf16[32,2,8192]{2,1,0:T(2,128)(2,1)}) %all-gather.5.cloned.1.call-update) | async-done | bytes 1048592 | tf_op jit(solution)/shard_map/while/body/eval_jaxpr/all_gather | solution.py:69
  277.6 1.8 reshape.96
  281.0 3.1 fusion.63
  285.0 6.0 convolution_convert_fusion.2
  293.4 111.5 %all-reduce.5.cloned.1.call-done = bf16[64,8192]{1,0:T(8,128)(2,1)} async-done(((bf16[64,8192]{1,0:T(8,128)(2,1)}), bf16[64,8192]{1,0:T(8,128)(2,1)}) %all-reduce.5.cloned.1.call-update) | async-done | bytes 1048592 | tf_op jit(solution)/shard_map/while
  407.3 3.4 collective-permute-done
  412.5 51.3 %all-gather.5.cloned.1.call-done = bf16[32,2,8192]{2,1,0:T(2,128)(2,1)} async-done(((bf16[1,2,8192]{2,1,0:T(2,128)(2,1)}), bf16[32,2,8192]{2,1,0:T(2,128)(2,1)}) %all-gather.5.cloned.1.call-update) | async-done | bytes 1048592 | tf_op jit(solution)/shard_map/while/body/eval_jaxpr/all_gather | solution.py:69
  463.7 1.8 reshape.96
  467.2 3.1 fusion.63
  471.2 6.0 convolution_convert_fusion.2
  479.5 111.5 %all-reduce.5.cloned.1.call-done = bf16[64,8192]{1,0:T(8,128)(2,1)} async-done(((bf16[64,8192]{1,0:T(8,128)(2,1)}), bf16[64,8192]{1,0:T(8,128)(2,1)}) %all-reduce.5.cloned.1.call-update) | async-done | bytes 1048592 | tf_op jit(solution)/shard_map/while
  593.4 3.4 collective-permute-done
  598.6 51.6 %all-gather.5.cloned.1.call-done = bf16[32,2,8192]{2,1,0:T(2,128)(2,1)} async-done(((bf16[1,2,8192]{2,1,0:T(2,128)(2,1)}), bf16[32,2,8192]{2,1,0:T(2,128)(2,1)}) %all-gather.5.cloned.1.call-update) | async-done | bytes 1048592 | tf_op jit(solution)/shard_map/while/body/eval_jaxpr/all_gather | solution.py:69
  650.2 1.8 reshape.96
  653.7 3.1 fusion.63
  657.7 6.0 convolution_convert_fusion.2
  666.0 111.5 %all-reduce.5.cloned.1.call-done = bf16[64,8192]{1,0:T(8,128)(2,1)} async-done(((bf16[64,8192]{1,0:T(8,128)(2,1)}), bf16[64,8192]{1,0:T(8,128)(2,1)}) %all-reduce.5.cloned.1.call-update) | async-done | bytes 1048592 | tf_op jit(solution)/shard_map/while
  779.9 3.4 collective-permute-done
  785.1 51.6 %all-gather.5.cloned.1.call-done = bf16[32,2,8192]{2,1,0:T(2,128)(2,1)} async-done(((bf16[1,2,8192]{2,1,0:T(2,128)(2,1)}), bf16[32,2,8192]{2,1,0:T(2,128)(2,1)}) %all-gather.5.cloned.1.call-update) | async-done | bytes 1048592 | tf_op jit(solution)/shard_map/while/body/eval_jaxpr/all_gather | solution.py:69
  836.7 1.8 reshape.96
  840.1 3.1 fusion.63
  844.1 6.0 convolution_convert_fusion.2
  852.5 111.5 %all-reduce.5.cloned.1.call-done = bf16[64,8192]{1,0:T(8,128)(2,1)} async-done(((bf16[64,8192]{1,0:T(8,128)(2,1)}), bf16[64,8192]{1,0:T(8,128)(2,1)}) %all-reduce.5.cloned.1.call-update) | async-done | bytes 1048592 | tf_op jit(solution)/shard_map/while
  966.4 3.4 collective-permute-done
  971.6 51.6 %all-gather.5.cloned.1.call-done = bf16[32,2,8192]{2,1,0:T(2,128)(2,1)} async-done(((bf16[1,2,8192]{2,1,0:T(2,128)(2,1)}), bf16[32,2,8192]{2,1,0:T(2,128)(2,1)}) %all-gather.5.cloned.1.call-update) | async-done | bytes 1048592 | tf_op jit(solution)/shard_map/while/body/eval_jaxpr/all_gather | solution.py:69
  1026.6 3.1 fusion.63
  1030.6 6.0 convolution_convert_fusion.2
  1038.9 111.6 %all-reduce.5.cloned.1.call-done = bf16[64,8192]{1,0:T(8,128)(2,1)} async-done(((bf16[64,8192]{1,0:T(8,128)(2,1)}), bf16[64,8192]{1,0:T(8,128)(2,1)}) %all-reduce.5.cloned.1.call-update) | async-done | bytes 1048592 | tf_op jit(solution)/shard_map/while
  1152.9 3.4 collective-permute-done
  1158.1 51.6 %all-gather.5.cloned.1.call-done = bf16[32,2,8192]{2,1,0:T(2,128)(2,1)} async-done(((bf16[1,2,8192]{2,1,0:T(2,128)(2,1)}), bf16[32,2,8192]{2,1,0:T(2,128)(2,1)}) %all-gather.5.cloned.1.call-update) | async-done | bytes 1048592 | tf_op jit(solution)/shard_map/while/body/eval_jaxpr/all_gather | solution.py:69
  1213.1 3.1 fusion.63
  1217.1 6.0 convolution_convert_fusion.2
  1225.5 111.6 %all-reduce.5.cloned.1.call-done = bf16[64,8192]{1,0:T(8,128)(2,1)} async-done(((bf16[64,8192]{1,0:T(8,128)(2,1)}), bf16[64,8192]{1,0:T(8,128)(2,1)}) %all-reduce.5.cloned.1.call-update) | async-done | bytes 1048592 | tf_op jit(solution)/shard_map/while
  1339.4 3.4 collective-permute-done
  1344.6 51.3 %all-gather.5.cloned.1.call-done = bf16[32,2,8192]{2,1,0:T(2,128)(2,1)} async-done(((bf16[1,2,8192]{2,1,0:T(2,128)(2,1)}), bf16[32,2,8192]{2,1,0:T(2,128)(2,1)}) %all-gather.5.cloned.1.call-update) | async-done | bytes 1048592 | tf_op jit(solution)/shard_map/while/body/eval_jaxpr/all_gather | solution.py:69
  1399.4 3.1 fusion.63
  1403.4 6.0 convolution_convert_fusion.2
  1411.7 111.5 %all-reduce.5.cloned.1.call-done = bf16[64,8192]{1,0:T(8,128)(2,1)} async-done(((bf16[64,8192]{1,0:T(8,128)(2,1)}), bf16[64,8192]{1,0:T(8,128)(2,1)}) %all-reduce.5.cloned.1.call-update) | async-done | bytes 1048592 | tf_op jit(solution)/shard_map/while
  1525.6 3.4 collective-permute-done
  1530.8 51.3 %all-gather.5.cloned.1.call-done = bf16[32,2,8192]{2,1,0:T(2,128)(2,1)} async-done(((bf16[1,2,8192]{2,1,0:T(2,128)(2,1)}), bf16[32,2,8192]{2,1,0:T(2,128)(2,1)}) %all-gather.5.cloned.1.call-update) | async-done | bytes 1048592 | tf_op jit(solution)/shard_map/while/body/eval_jaxpr/all_gather | solution.py:69
  1582.1 1.8 reshape.96
  1585.5 3.1 fusion.63
  1589.5 6.0 convolution_convert_fusion.2
  1597.9 111.6 %all-reduce.5.cloned.1.call-done = bf16[64,8192]{1,0:T(8,128)(2,1)} async-done(((bf16[64,8192]{1,0:T(8,128)(2,1)}), bf16[64,8192]{1,0:T(8,128)(2,1)}) %all-reduce.5.cloned.1.call-update) | async-done | bytes 1048592 | tf_op jit(solution)/shard_map/while
  1711.8 3.4 collective-permute-done
  1717.0 51.6 %all-gather.5.cloned.1.call-done = bf16[32,2,8192]{2,1,0:T(2,128)(2,1)} async-done(((bf16[1,2,8192]{2,1,0:T(2,128)(2,1)}), bf16[32,2,8192]{2,1,0:T(2,128)(2,1)}) %all-gather.5.cloned.1.call-update) | async-done | bytes 1048592 | tf_op jit(solution)/shard_map/while/body/eval_jaxpr/all_gather | solution.py:69
  1772.1 3.1 fusion.63
  1776.1 6.0 convolution_convert_fusion.2
  1784.4 111.6 %all-reduce.5.cloned.1.call-done = bf16[64,8192]{1,0:T(8,128)(2,1)} async-done(((bf16[64,8192]{1,0:T(8,128)(2,1)}), bf16[64,8192]{1,0:T(8,128)(2,1)}) %all-reduce.5.cloned.1.call-update) | async-done | bytes 1048592 | tf_op jit(solution)/shard_map/while
  1898.3 3.4 collective-permute-done
  1903.5 51.6 %all-gather.5.cloned.1.call-done = bf16[32,2,8192]{2,1,0:T(2,128)(2,1)} async-done(((bf16[1,2,8192]{2,1,0:T(2,128)(2,1)}), bf16[32,2,8192]{2,1,0:T(2,128)(2,1)}) %all-gather.5.cloned.1.call-update) | async-done | bytes 1048592 | tf_op jit(solution)/shard_map/while/body/eval_jaxpr/all_gather | solution.py:69
  1958.6 3.1 fusion.63
  1962.6 6.0 convolution_convert_fusion.2
  1970.9 111.6 %all-reduce.5.cloned.1.call-done = bf16[64,8192]{1,0:T(8,128)(2,1)} async-done(((bf16[64,8192]{1,0:T(8,128)(2,1)}), bf16[64,8192]{1,0:T(8,128)(2,1)}) %all-reduce.5.cloned.1.call-update) | async-done | bytes 1048592 | tf_op jit(solution)/shard_map/while
  2084.9 3.4 collective-permute-done
  (250 shorter events, 101.5 us)
Async XLA Ops:
  15.0 23.6 %copy-start.2 = (s32[1,4,28]{2,1,0:T(4,128)S(1)}, s32[1,4,28]{2,1,0:T(4,128)}, u32[]{:S(2)}) copy-start(s32[1,4,28]{2,1,0:T(4,128)} %param.15) | copy-start | bytes 1348
  15.0 23.8 %copy-start = (f32[1,8192]{1,0:T(1,128)S(1)}, f32[1,8192]{1,0:T(1,128)}, u32[]{:S(2)}) copy-start(f32[1,8192]{1,0:T(1,128)} %param.12) | copy-start | bytes 98308
  15.0 23.8 %copy-start.4 = (s32[4]{0:T(128)S(1)}, s32[4]{0:T(128)}, u32[]{:S(2)}) copy-start(s32[4]{0:T(128)} %param.11) | copy-start | bytes 52
  15.0 23.8 %copy-start.5 = (u32[256]{0:T(256)S(1)}, u32[256]{0:T(256)}, u32[]{:S(2)}) copy-start(u32[256]{0:T(256)} %constant.220) | copy-start | bytes 3076
  39.0 52.1 %all-gather.5.cloned.1.call-start = ((), (), s32[]{:S(2)}) async-start(), calls=%async_computation | async-start | bytes 1081344 | tf_op jit(solution)/shard_map/while/body/eval_jaxpr/all_gather | solution.py:69
  40.8 177.7 %all-reduce.5.cloned.1.call-start = ((), (), s32[]{:S(2)}) async-start(), calls=%async_computation.1 | async-start | bytes 2097152 | tf_op jit(solution)/shard_map/while
  94.6 3.1 copy-start.3
  219.5 4.7 collective-permute-start
  224.1 53.4 %all-gather.5.cloned.1.call-start = ((), (), s32[]{:S(2)}) async-start(), calls=%async_computation | async-start | bytes 1081344 | tf_op jit(solution)/shard_map/while/body/eval_jaxpr/all_gather | solution.py:69
  225.8 179.1 %all-reduce.5.cloned.1.call-start = ((), (), s32[]{:S(2)}) async-start(), calls=%async_computation.1 | async-start | bytes 2097152 | tf_op jit(solution)/shard_map/while
  281.0 3.1 copy-start.3
  406.0 4.7 collective-permute-start
  410.6 53.1 %all-gather.5.cloned.1.call-start = ((), (), s32[]{:S(2)}) async-start(), calls=%async_computation | async-start | bytes 1081344 | tf_op jit(solution)/shard_map/while/body/eval_jaxpr/all_gather | solution.py:69
  412.3 178.8 %all-reduce.5.cloned.1.call-start = ((), (), s32[]{:S(2)}) async-start(), calls=%async_computation.1 | async-start | bytes 2097152 | tf_op jit(solution)/shard_map/while
  467.2 3.1 copy-start.3
  592.1 4.7 collective-permute-start
  596.8 53.4 %all-gather.5.cloned.1.call-start = ((), (), s32[]{:S(2)}) async-start(), calls=%async_computation | async-start | bytes 1081344 | tf_op jit(solution)/shard_map/while/body/eval_jaxpr/all_gather | solution.py:69
  598.5 179.1 %all-reduce.5.cloned.1.call-start = ((), (), s32[]{:S(2)}) async-start(), calls=%async_computation.1 | async-start | bytes 2097152 | tf_op jit(solution)/shard_map/while
  653.7 3.1 copy-start.3
  778.6 4.7 collective-permute-start
  783.2 53.4 %all-gather.5.cloned.1.call-start = ((), (), s32[]{:S(2)}) async-start(), calls=%async_computation | async-start | bytes 1081344 | tf_op jit(solution)/shard_map/while/body/eval_jaxpr/all_gather | solution.py:69
  784.9 179.1 %all-reduce.5.cloned.1.call-start = ((), (), s32[]{:S(2)}) async-start(), calls=%async_computation.1 | async-start | bytes 2097152 | tf_op jit(solution)/shard_map/while
  840.1 3.1 copy-start.3
  965.1 4.7 collective-permute-start
  969.7 53.4 %all-gather.5.cloned.1.call-start = ((), (), s32[]{:S(2)}) async-start(), calls=%async_computation | async-start | bytes 1081344 | tf_op jit(solution)/shard_map/while/body/eval_jaxpr/all_gather | solution.py:69
  971.4 179.1 %all-reduce.5.cloned.1.call-start = ((), (), s32[]{:S(2)}) async-start(), calls=%async_computation.1 | async-start | bytes 2097152 | tf_op jit(solution)/shard_map/while
  1026.6 3.1 copy-start.3
  1151.6 4.7 collective-permute-start
  1156.2 53.4 %all-gather.5.cloned.1.call-start = ((), (), s32[]{:S(2)}) async-start(), calls=%async_computation | async-start | bytes 1081344 | tf_op jit(solution)/shard_map/while/body/eval_jaxpr/all_gather | solution.py:69
  1157.9 179.1 %all-reduce.5.cloned.1.call-start = ((), (), s32[]{:S(2)}) async-start(), calls=%async_computation.1 | async-start | bytes 2097152 | tf_op jit(solution)/shard_map/while
  1213.1 3.1 copy-start.3
  1338.1 4.7 collective-permute-start
  1342.8 53.1 %all-gather.5.cloned.1.call-start = ((), (), s32[]{:S(2)}) async-start(), calls=%async_computation | async-start | bytes 1081344 | tf_op jit(solution)/shard_map/while/body/eval_jaxpr/all_gather | solution.py:69
  1344.5 178.8 %all-reduce.5.cloned.1.call-start = ((), (), s32[]{:S(2)}) async-start(), calls=%async_computation.1 | async-start | bytes 2097152 | tf_op jit(solution)/shard_map/while
  1399.4 3.1 copy-start.3
  1524.3 4.7 collective-permute-start
  1528.9 53.1 %all-gather.5.cloned.1.call-start = ((), (), s32[]{:S(2)}) async-start(), calls=%async_computation | async-start | bytes 1081344 | tf_op jit(solution)/shard_map/while/body/eval_jaxpr/all_gather | solution.py:69
  1530.6 178.8 %all-reduce.5.cloned.1.call-start = ((), (), s32[]{:S(2)}) async-start(), calls=%async_computation.1 | async-start | bytes 2097152 | tf_op jit(solution)/shard_map/while
  1585.5 3.1 copy-start.3
  1710.5 4.7 collective-permute-start
  1715.2 53.4 %all-gather.5.cloned.1.call-start = ((), (), s32[]{:S(2)}) async-start(), calls=%async_computation | async-start | bytes 1081344 | tf_op jit(solution)/shard_map/while/body/eval_jaxpr/all_gather | solution.py:69
  1716.9 179.1 %all-reduce.5.cloned.1.call-start = ((), (), s32[]{:S(2)}) async-start(), calls=%async_computation.1 | async-start | bytes 2097152 | tf_op jit(solution)/shard_map/while
  1772.0 3.1 copy-start.3
  1897.0 4.7 collective-permute-start
  1901.7 53.4 %all-gather.5.cloned.1.call-start = ((), (), s32[]{:S(2)}) async-start(), calls=%async_computation | async-start | bytes 1081344 | tf_op jit(solution)/shard_map/while/body/eval_jaxpr/all_gather | solution.py:69
  1903.4 179.1 %all-reduce.5.cloned.1.call-start = ((), (), s32[]{:S(2)}) async-start(), calls=%async_computation.1 | async-start | bytes 2097152 | tf_op jit(solution)/shard_map/while
  1958.6 3.1 copy-start.3
  2083.6 4.7 collective-permute-start
  2088.2 0.7 copy-start.1
Sparse Core Ops, SparseCore 0:
  42.4 48.6 all-gather.4
  104.7 113.7 all-reduce.4
  227.5 50.0 all-gather.4
  291.1 113.7 all-reduce.4
  413.7 50.0 all-gather.4
  477.3 113.7 all-reduce.4
  600.2 50.0 all-gather.4
  663.8 113.7 all-reduce.4
  786.6 50.0 all-gather.4
  850.2 113.7 all-reduce.4
  973.1 50.0 all-gather.4
  1036.7 113.7 all-reduce.4
  1159.6 50.0 all-gather.4
  1223.2 113.8 all-reduce.4
  1345.8 50.0 all-gather.4
  1409.5 113.7 all-reduce.4
  1532.0 50.0 all-gather.4
  1595.6 113.7 all-reduce.4
  1718.5 50.0 all-gather.4
  1782.2 113.7 all-reduce.4
  1905.1 50.0 all-gather.4
  1968.7 113.7 all-reduce.4
where the time goes:
time: 2100 us
  waiting for transfers between devices  1830 us (87%)
  matrix products  118 us (6%)
  local copies, waits for them, and re-layouts  75.8 us (4%)
  other arithmetic  36 us (2%)
    while x33, waiting for transfers between devices  1230 us
    all_gather x11, waiting for transfers between devices, turn_step(): hidden = expand(lax.all_gather(normed, 'shard', axis=0, tiled=True))  565 us
    dot_general x11, matrix products, turn_step(): jnp.dot(hidden, dense_down, preferred_element_type=jnp.float32)  65.5 us
  transfers between devices with their start and end apart: 33, of which 33 were waited for; matrix products, arithmetic and copies ran while one was open for 1% of the time, Pallas kernels for 0%

commit v1 on v0

v1 whole, which is shorter than its diff:
```python
import functools

import jax
import jax.numpy as jnp
from jax import lax
from jax.experimental import pallas as pl
from jax.experimental.pallas import tpu as pltpu
from jax.sharding import PartitionSpec as P

NORM_EPS = 1e-05
LIVE = 160
ROWS = 16
UNITS = LIVE // ROWS
SIDE = 4
CHIPS = SIDE * SIDE
SECTIONS = 8
BLOCK = 128
NB = 64
HALF = NB // 2
HB = 4
KMAX = 28
MESH = pl.DeviceIdType.MESH
SEND_ORDER = sorted(range(CHIPS), key=lambda step: -sum(min(d, SIDE - d) for d in divmod(step, SIDE)))


def kernel(
    lengths, in_index, inverse, tokens, gain, gate, up, down, out,
    gate_up, down_tiles, down_dense, gathered, normed, given, kept, core_got, summed, got, first, result,
    row_send, row_got, out_send, out_got,
    load_sem, gather_sem, gather_sent, core_sem, core_sent, pair_sem, pair_sent,
    scatter_sem, scatter_sent, first_sent, row_sem, row_sent, out_sem, out_sent,
):
    section = lax.axis_index("section")
    shard = lax.axis_index("shard")
    chip = shard // 2
    core = shard % 2
    chip_y = chip // SIDE
    chip_x = chip % SIDE
    half = core * HALF
    other_half = HALF - half
    own = half + chip * 2
    partner = (section, chip * 2 + 1 - core)

    loads = []
    for j in range(HB):
        loads.append(pltpu.make_async_copy(gate.at[j], gate_up.at[j, :, pl.ds(0, BLOCK)], load_sem.at[0, j]))
        loads.append(pltpu.make_async_copy(up.at[j], gate_up.at[j, :, pl.ds(BLOCK, BLOCK)], load_sem.at[1, j]))
        loads.append(pltpu.make_async_copy(down.at[j], down_tiles.at[j, pl.ds(0, KMAX)], load_sem.at[2, j]))
    for load in loads:
        load.start()

    def chip_at(step):
        return (chip_y + step // SIDE) % SIDE * SIDE + (chip_x + step % SIDE) % SIDE

    barrier = pltpu.get_barrier_semaphore()
    before = (section + SECTIONS - 1) % SECTIONS

    def greet_plane(step, carry):
        pl.semaphore_signal(barrier, inc=1, device_id=(section, (shard + step) % 32), device_id_type=MESH)
        return carry

    def greet_before(step, carry):
        pl.semaphore_signal(barrier, inc=1, device_id=(before, step * 2 + core), device_id_type=MESH)
        return carry

    lax.fori_loop(1, 32, greet_plane, 0)
    lax.fori_loop(0, CHIPS, greet_before, 0)
    pl.semaphore_wait(barrier, 31 + CHIPS)

    offsets = [jnp.int32(0)]
    for m in range(3):
        offsets.append(offsets[-1] + lengths[m])

    def position(index):
        block = (index >> 3) & 1
        micro = (index >> 1) & 3
        row = (index >> 4) * 2 + (index & 1)
        start = jnp.full_like(index, 0)
        length = jnp.full_like(index, lengths[0])
        for m in range(1, 4):
            start = jnp.where(micro == m, offsets[m], start)
            length = jnp.where(micro == m, lengths[m], length)
        return jnp.where(row < length, start + row, -1), block

    @pl.when(section == 0)
    def _():
        for b in range(NB):
            owner = b % HALF // 2 * 2 + b // HALF
            row_send[owner, pl.ds(b % 2 * 8, 8), :] = tokens[:, pl.ds(b * BLOCK, BLOCK)]
        pltpu.make_async_copy(row_send.at[shard], row_got.at[shard], row_sem).start()

        def send_rows(step, carry):
            there = (shard + step) % 32
            pltpu.make_async_remote_copy(
                row_send.at[there], row_got.at[shard], row_sent, row_sem, device_id=(section, there), device_id_type=MESH
            ).start()
            return carry

        lax.fori_loop(1, 32, send_rows, 0)
        pltpu.make_async_copy(row_got, row_got, row_sem).wait()
        where, block = position(lax.broadcasted_iota(jnp.int32, (LIVE, 512), 1))
        at = lax.broadcasted_iota(jnp.int32, (LIVE, 512), 0)
        rows = row_got[...].reshape(512, BLOCK)
        for b in range(2):
            pick = jnp.where((where == at) & (block == b), 1.0, 0.0).astype(jnp.bfloat16)
            compact = jnp.dot(pick, rows, preferred_element_type=jnp.float32).astype(jnp.bfloat16)
            first[:, b] = compact.reshape(UNITS, ROWS, BLOCK)

        def send_first(unit, carry):
            pltpu.make_async_copy(first.at[unit], gathered.at[unit, pl.ds(own, 2)], gather_sem.at[unit]).start()
            for step in SEND_ORDER[:-1]:
                pltpu.make_async_remote_copy(
                    first.at[unit],
                    gathered.at[unit, pl.ds(own, 2)],
                    first_sent.at[unit],
                    gather_sem.at[unit],
                    device_id=(section, chip_at(step) * 2 + core),
                    device_id_type=MESH,
                ).start()
            return carry

        pltpu.make_async_copy(row_got.at[pl.ds(0, 31)], row_got.at[pl.ds(0, 31)], row_sent).wait()
        lax.fori_loop(0, UNITS, send_first, 0)

    for load in loads:
        load.wait()
    zero_tile = jnp.zeros((BLOCK, BLOCK), jnp.bfloat16)
    for j in range(HB):
        down_tiles[j, KMAX] = zero_tile
    normed[NB] = jnp.zeros((ROWS, BLOCK), jnp.bfloat16)

    def widen(block, carry):
        columns = pl.ds(pl.multiple_of(block * BLOCK, BLOCK), BLOCK)
        for side, start in ((0, other_half), (1, half)):
            for j in range(HB):
                down_dense[side, pl.ds(j * BLOCK, BLOCK), columns] = down_tiles[j, inverse[j, start + block]]
        return carry

    lax.fori_loop(0, HALF, widen, 0)

    def work(unit):
        mine = gathered.at[unit, pl.ds(half, HALF)]
        theirs = gathered.at[unit, pl.ds(other_half, HALF)]
        pltpu.make_async_copy(mine, mine, gather_sem.at[unit]).wait()
        pltpu.make_async_remote_copy(
            mine, mine, core_sent.at[unit], core_sem.at[unit], device_id=partner, device_id_type=MESH
        ).start()

        squares = jnp.zeros((ROWS, BLOCK), jnp.float32)

        def scale(start, squares):
            for b in range(HALF):
                x = gathered[unit, start + b].astype(jnp.float32)
                squares = squares + x * x
                columns = pl.ds(pl.multiple_of((start + b) * BLOCK, BLOCK), BLOCK)
                normed[start + b] = (x * gain[0:1, columns]).astype(jnp.bfloat16)
            return squares

        squares = scale(half, squares)
        pltpu.make_async_copy(theirs, theirs, core_sem.at[unit]).wait()
        squares = scale(other_half, squares)
        mean = jnp.sum(squares, axis=-1, keepdims=True) * (1.0 / (NB * BLOCK))
        row_scale = lax.rsqrt(mean + NORM_EPS)

        hidden = []
        for j in range(HB):
            picked = []
            for k in range(KMAX):
                slot = in_index[j, k]
                picked.append(normed[jnp.where(slot < 0, NB, slot)])
            both = jnp.dot(
                jnp.concatenate(picked, axis=1), gate_up[j], preferred_element_type=jnp.float32
            )
            gate_val = both[:, :BLOCK] * row_scale
            up_val = both[:, BLOCK:] * row_scale
            hidden.append((gate_val / (1.0 + jnp.exp(-gate_val)) * up_val).astype(jnp.bfloat16))
        hidden = jnp.concatenate(hidden, axis=1)

        partial = jnp.dot(hidden, down_dense[0], preferred_element_type=jnp.float32)
        for b in range(HALF):
            given[unit, b] = partial[:, b * BLOCK : (b + 1) * BLOCK].astype(jnp.bfloat16)
        pltpu.make_async_remote_copy(
            given.at[unit], core_got.at[unit], pair_sent.at[unit], pair_sem.at[unit], device_id=partner, device_id_type=MESH
        ).start()
        partial = jnp.dot(hidden, down_dense[1], preferred_element_type=jnp.float32)
        for b in range(HALF):
            kept[b] = partial[:, b * BLOCK : (b + 1) * BLOCK]
        pltpu.make_async_copy(core_got.at[unit], core_got.at[unit], pair_sem.at[unit]).wait()
        for b in range(HALF):
            summed[unit, b] = (kept[b] + core_got[unit, b].astype(jnp.float32)).astype(jnp.bfloat16)
        for step in SEND_ORDER[:-1]:
            there = chip_at(step)
            pltpu.make_async_remote_copy(
                summed.at[unit, pl.ds(there * 2, 2)],
                got.at[unit, chip],
                scatter_sent.at[unit],
                scatter_sem.at[unit],
                device_id=(section, there * 2 + core),
                device_id_type=MESH,
            ).start()
        pltpu.make_async_copy(
            summed.at[unit, pl.ds(chip * 2, 2)], got.at[unit, chip], scatter_sem.at[unit]
        ).start()

    def finish(unit):
        pltpu.make_async_copy(got.at[unit], got.at[unit], scatter_sem.at[unit]).wait()
        for b in range(2):
            total = got[unit, 0, b].astype(jnp.float32)
            for c in range(1, CHIPS):
                total = total + got[unit, c, b].astype(jnp.float32)
            result[unit, b] = (gathered[unit, own + b].astype(jnp.float32) + total).astype(jnp.bfloat16)

        @pl.when(section < SECTIONS - 1)
        def _():
            for step in SEND_ORDER:
                pltpu.make_async_remote_copy(
                    result.at[unit],
                    gathered.at[unit, pl.ds(own, 2)],
                    gather_sent.at[unit],
                    gather_sem.at[unit],
                    device_id=(section + 1, chip_at(step) * 2 + core),
                    device_id_type=MESH,
                ).start()

    def turn(unit, carry):
        @pl.when(unit < UNITS)
        def _():
            work(unit)

        @pl.when(unit > 0)
        def _():
            finish(unit - 1)

        return carry

    lax.fori_loop(0, UNITS + 1, turn, 0)

    where, block = position(lax.broadcasted_iota(jnp.int32, (512, LIVE), 0))
    at = lax.broadcasted_iota(jnp.int32, (512, LIVE), 1)
    spread = jnp.zeros((512, BLOCK), jnp.float32)
    for b in range(2):
        place = jnp.where((where == at) & (block == b), 1.0, 0.0).astype(jnp.bfloat16)
        spread = spread + jnp.dot(place, result[:, b].reshape(LIVE, BLOCK), preferred_element_type=jnp.float32)
    out_send[...] = spread.astype(jnp.bfloat16).reshape(32, 16, BLOCK)
    pltpu.make_async_copy(out_send.at[shard], out_got.at[shard], out_sem).start()

    def send_out(step, carry):
        there = (shard + step) % 32
        pltpu.make_async_remote_copy(
            out_send.at[there], out_got.at[shard], out_sent, out_sem, device_id=(section, there), device_id_type=MESH
        ).start()
        return carry

    lax.fori_loop(1, 32, send_out, 0)

    def drain(unit, carry):
        mine = gathered.at[unit, pl.ds(half, HALF)]
        sent = got.at[unit, pl.ds(0, CHIPS - 1)]
        pltpu.make_async_copy(mine, mine, core_sent.at[unit]).wait()
        pltpu.make_async_copy(given.at[unit], given.at[unit], pair_sent.at[unit]).wait()
        pltpu.make_async_copy(sent, sent, scatter_sent.at[unit]).wait()

        @pl.when(section < SECTIONS - 1)
        def _():
            pltpu.make_async_copy(got.at[unit], got.at[unit], gather_sent.at[unit]).wait()

        @pl.when(section == 0)
        def _():
            pltpu.make_async_copy(sent, sent, first_sent.at[unit]).wait()

        return carry

    lax.fori_loop(0, UNITS, drain, 0)
    pltpu.make_async_copy(out_got, out_got, out_sem).wait()
    for b in range(NB):
        owner = b % HALF // 2 * 2 + b // HALF
        out[:, pl.ds(b * BLOCK, BLOCK)] = out_got[owner, pl.ds(b % 2 * 8, 8), :]
    pltpu.make_async_copy(out_got.at[pl.ds(0, 31)], out_got.at[pl.ds(0, 31)], out_sent).wait()


def body(tokens, lengths, norm_gain, gate_tiles, up_tiles, in_index, down_tiles, out_index):
    slots = jnp.arange(KMAX, dtype=jnp.int32)
    hit = out_index[0][:, None, :] == jnp.arange(NB, dtype=jnp.int32)[None, :, None]
    inverse = jnp.min(jnp.where(hit, slots, KMAX), axis=-1)
    bf16 = functools.partial(pltpu.VMEM, dtype=jnp.bfloat16)
    dma = pltpu.SemaphoreType.DMA
    smem = pl.BlockSpec(memory_space=pltpu.SMEM)
    vmem = pl.BlockSpec(memory_space=pltpu.VMEM)
    hbm = pl.BlockSpec(memory_space=pl.ANY)
    rows = pl.pallas_call(
        kernel,
        out_shape=jax.ShapeDtypeStruct((8, NB * BLOCK), jnp.bfloat16),
        in_specs=[smem, smem, smem, vmem, vmem, hbm, hbm, hbm],
        out_specs=vmem,
        scratch_shapes=[
            bf16((HB, KMAX * BLOCK, 2 * BLOCK)),
            bf16((HB, KMAX + 1, BLOCK, BLOCK)),
            bf16((2, HB * BLOCK, HALF * BLOCK)),
            bf16((UNITS, NB, ROWS, BLOCK)),
            bf16((NB + 1, ROWS, BLOCK)),
            bf16((UNITS, HALF, ROWS, BLOCK)),
            pltpu.VMEM((HALF, ROWS, BLOCK), jnp.float32),
            bf16((UNITS, HALF, ROWS, BLOCK)),
            bf16((UNITS, HALF, ROWS, BLOCK)),
            bf16((UNITS, CHIPS, 2, ROWS, BLOCK)),
            bf16((UNITS, 2, ROWS, BLOCK)),
            bf16((UNITS, 2, ROWS, BLOCK)),
            bf16((32, 16, BLOCK)),
            bf16((32, 16, BLOCK)),
            bf16((32, 16, BLOCK)),
            bf16((32, 16, BLOCK)),
            dma((3, HB)),
            dma((UNITS,)),
            dma((UNITS,)),
            dma((UNITS,)),
            dma((UNITS,)),
            dma((UNITS,)),
            dma((UNITS,)),
            dma((UNITS,)),
            dma((UNITS,)),
            dma((UNITS,)),
            dma,
            dma,
            dma,
            dma,
        ],
        compiler_params=pltpu.CompilerParams(
            collective_id=0, has_side_effects=True, vmem_limit_bytes=52 * 1024 * 1024
        ),
        name="relay",
    )(
        lengths,
        in_index[0],
        inverse,
        tokens.reshape(8, NB * BLOCK),
        norm_gain,
        gate_tiles.reshape(HB, KMAX * BLOCK, BLOCK),
        up_tiles.reshape(HB, KMAX * BLOCK, BLOCK),
        down_tiles.reshape(HB, KMAX, BLOCK, BLOCK),
    )
    return rows.reshape(1, 4, 2, NB * BLOCK)


def solution(mesh):
    placed = (
        P(None, "shard", None),
        P(),
        P("section", None),
        P("section", "shard", None, None, None),
        P("section", "shard", None, None, None),
        P("section", "shard", None),
        P("section", "shard", None, None, None),
        P("section", "shard", None),
    )
    return jax.shard_map(
        body,
        mesh=mesh,
        in_specs=placed,
        out_specs=P("section", None, "shard", None),
        check_vma=False,
    )
```

time: 2100 us -> 189 us (0.09)
  waiting for transfers between devices: 1830 us -> 0 us
  Pallas kernels: 0 us -> 184 us
  matrix products: 118 us -> 0 us
  local copies, waits for them, and re-layouts: 75.8 us -> 4.58 us
  other arithmetic: 36 us -> 0.1 us
    while x33 -> x0, waiting for transfers between devices: 1230 us -> none
    all_gather x11 -> x0, waiting for transfers between devices: 565 us -> none  [turn_step(): hidden = expand(lax.all_gather(normed, 'shard', axis=0, tiled=True))]
    pallas_call x0 -> x1, Pallas kernels: none -> 184 us  [body(): pl.pallas_call(kernel, out_shape=jax.ShapeDtypeStruct((8, NB * BLOCK), jn...]
    dot_general x34 -> x0, matrix products: 118 us -> none  [the longest x11 65.5 us: turn_step(): jnp.dot(hidden, dense_down, preferred_element_type=jnp.float32)]
    ppermute x11 -> x0, waiting for transfers between devices: 36.9 us -> none  [shifted(): return lax.ppermute(value, axis, pairs)]
    reshape x22 -> x2, local copies, waits for them, and re-layouts: 27.8 us -> 1.72 us  [the longest x1 0.96 us: body(): tokens.reshape(8, NB * BLOCK)]
    unnamed x11 -> x6, local copies, waits for them, and re-layouts: 24.3 us -> 2.09 us
  transfers between devices with their start and end apart: 33 -> 0, of which waited for: 33 -> 0; matrix products, arithmetic and copies ran while one was open for 1% -> 0% of each run, Pallas kernels for 0% -> 0%
where the time goes in v1:
time: 189 us
  Pallas kernels  184 us (97%)
  local copies, waits for them, and re-layouts  4.58 us (2%)
    pallas_call x1, Pallas kernels, body(): pl.pallas_call(kernel, out_shape=jax.ShapeDtypeStruct((8, NB * BLOCK), jn...  184 us

profile of v1, /device:TPU:225, one launch (start us, length us, event | category | flops | bytes accessed | tf_op | source)
XLA Modules:
  0.0 189.2 jit_solution(13557277737771639879)
XLA Ops:
  0.0 0.8 copy.9
  0.8 0.1 select_reduce_fusion.inverse
  0.9 1.0 reshape.16.tokens
  1.8 0.0 copy-start
  1.9 0.7 copy-done
  2.6 0.0 copy-start.1
  2.6 0.7 copy-done.1
  3.3 0.0 copy-start.2
  3.3 0.7 copy-done.2
  3.9 184.5 %relay.1 = bf16[8,8192]{1,0:T(8,128)(2,1)S(1)} custom-call(s32[4]{0:T(128)S(1)} %copy-done.2, s32[4,28]{1,0:T(4,128)S(1)} %bitcast.5, s32[4,64]{1,0:T(4,128)S(1)} %select_reduce_fusion.inverse, bf16[8,8192]{1,0:T(8,128)(2,1)S(1)} %reshape.16.tokens, f32[1,8192]{1,0:T(1,128)S(1)} %copy-done, bf16[4,3584,128]{2,1,0:T(8,128)(2,1)} %bitcast.6, ...), custom_call_target="tpu_custom_call" | custom-call | tf_op jit(solution)/shard_map/relay/pallas_call | solution.py:290
  188.4 0.8 reshape.20
Async XLA Ops:
  1.8 0.8 copy-start
  2.6 0.7 copy-start.1
  3.3 0.7 copy-start.2

commit v2 on v1

--- a/solution.py
+++ b/solution.py
@@ -19,15 +19,18 @@
 HALF = NB // 2
 HB = 4
 KMAX = 28
+LAG = 3
+LEAD = 4
 MESH = pl.DeviceIdType.MESH
 SEND_ORDER = sorted(range(CHIPS), key=lambda step: -sum(min(d, SIDE - d) for d in divmod(step, SIDE)))
 
 
 def kernel(
-    lengths, in_index, inverse, tokens, gain, gate, up, down, out,
-    gate_up, down_tiles, down_dense, gathered, normed, given, kept, core_got, summed, got, first, result,
+    lengths_in, in_index_in, out_index_in, tokens_in, gain_in, gate, up, down, out,
+    lengths, in_index, out_index, inverse, inverse_rows, tokens, gain,
+    gate_up, down_tiles, parts, gathered, normed, given, kept, core_got, summed, got, first, result,
     row_send, row_got, out_send, out_got,
-    load_sem, gather_sem, gather_sent, core_sem, core_sent, pair_sem, pair_sent,
+    small_sem, load_sem, gather_sem, gather_sent, core_sem, core_sent, pair_sem, pair_sent,
     scatter_sem, scatter_sent, first_sent, row_sem, row_sent, out_sem, out_sent,
 ):
     section = lax.axis_index("section")
@@ -41,11 +44,20 @@
     own = half + chip * 2
     partner = (section, chip * 2 + 1 - core)
 
+    smalls = [
+        pltpu.make_async_copy(lengths_in, lengths, small_sem.at[0]),
+        pltpu.make_async_copy(in_index_in, in_index, small_sem.at[1]),
+        pltpu.make_async_copy(out_index_in, out_index, small_sem.at[2]),
+        pltpu.make_async_copy(tokens_in, tokens, small_sem.at[3]),
+        pltpu.make_async_copy(gain_in, gain, small_sem.at[4]),
+    ]
+    for small in smalls:
+        small.start()
     loads = []
     for j in range(HB):
         loads.append(pltpu.make_async_copy(gate.at[j], gate_up.at[j, :, pl.ds(0, BLOCK)], load_sem.at[0, j]))
         loads.append(pltpu.make_async_copy(up.at[j], gate_up.at[j, :, pl.ds(BLOCK, BLOCK)], load_sem.at[1, j]))
-        loads.append(pltpu.make_async_copy(down.at[j], down_tiles.at[j, pl.ds(0, KMAX)], load_sem.at[2, j]))
+        loads.append(pltpu.make_async_copy(down.at[j], down_tiles.at[j], load_sem.at[2, j]))
     for load in loads:
         load.start()
 
@@ -65,8 +77,9 @@
 
     lax.fori_loop(1, 32, greet_plane, 0)
     lax.fori_loop(0, CHIPS, greet_before, 0)
-    pl.semaphore_wait(barrier, 31 + CHIPS)
-
+
+    for small in smalls:
+        small.wait()
     offsets = [jnp.int32(0)]
     for m in range(3):
         offsets.append(offsets[-1] + lengths[m])
@@ -82,11 +95,30 @@
             length = jnp.where(micro == m, lengths[m], length)
         return jnp.where(row < length, start + row, -1), block
 
+    blocks = lax.broadcasted_iota(jnp.int32, (1, BLOCK), 1)
+    for j in range(HB):
+        row = jnp.full((1, BLOCK), KMAX, jnp.int32)
+        for k in range(KMAX):
+            row = jnp.where(blocks == out_index[0, j, k], k, row)
+        inverse_rows[j : j + 1, :] = row
+    inverse_copy = pltpu.make_async_copy(inverse_rows, inverse, small_sem.at[5])
+    inverse_copy.start()
+    for j in range(HB):
+        parts[j, KMAX] = jnp.zeros((ROWS, BLOCK), jnp.float32)
+    normed[NB] = jnp.zeros((ROWS, BLOCK), jnp.bfloat16)
+
     @pl.when(section == 0)
     def _():
         for b in range(NB):
             owner = b % HALF // 2 * 2 + b // HALF
-            row_send[owner, pl.ds(b % 2 * 8, 8), :] = tokens[:, pl.ds(b * BLOCK, BLOCK)]
+            rows = [tokens[m, :, pl.ds(b * BLOCK, BLOCK)].astype(jnp.float32) for m in range(4)]
+            row_send[owner, pl.ds(b % 2 * 8, 8), :] = jnp.concatenate(rows, axis=0).astype(jnp.bfloat16)
+
+    inverse_copy.wait()
+    pl.semaphore_wait(barrier, 31 + CHIPS)
+
+    @pl.when(section == 0)
+    def _():
         pltpu.make_async_copy(row_send.at[shard], row_got.at[shard], row_sem).start()
 
         def send_rows(step, carry):
@@ -97,94 +129,97 @@
             return carry
 
         lax.fori_loop(1, 32, send_rows, 0)
-        pltpu.make_async_copy(row_got, row_got, row_sem).wait()
+
+    for load in loads:
+        load.wait()
+
+    def send_first(unit):
+        pltpu.make_async_copy(first.at[unit], gathered.at[unit, pl.ds(own, 2)], gather_sem.at[unit]).start()
+        for step in SEND_ORDER[:-1]:
+            pltpu.make_async_remote_copy(
+                first.at[unit],
+                gathered.at[unit, pl.ds(own, 2)],
+                first_sent.at[unit],
+                gather_sem.at[unit],
+                device_id=(section, chip_at(step) * 2 + core),
+                device_id_type=MESH,
+            ).start()
+
+    @pl.when(section == 0)
+    def _():
         where, block = position(lax.broadcasted_iota(jnp.int32, (LIVE, 512), 1))
         at = lax.broadcasted_iota(jnp.int32, (LIVE, 512), 0)
+        picks = [jnp.where((where == at) & (block == b), 1.0, 0.0).astype(jnp.bfloat16) for b in range(2)]
+        pltpu.make_async_copy(row_got, row_got, row_sem).wait()
         rows = row_got[...].reshape(512, BLOCK)
         for b in range(2):
-            pick = jnp.where((where == at) & (block == b), 1.0, 0.0).astype(jnp.bfloat16)
-            compact = jnp.dot(pick, rows, preferred_element_type=jnp.float32).astype(jnp.bfloat16)
+            compact = jnp.dot(picks[b], rows, preferred_element_type=jnp.float32).astype(jnp.bfloat16)
             first[:, b] = compact.reshape(UNITS, ROWS, BLOCK)
-
-        def send_first(unit, carry):
-            pltpu.make_async_copy(first.at[unit], gathered.at[unit, pl.ds(own, 2)], gather_sem.at[unit]).start()
-            for step in SEND_ORDER[:-1]:
-                pltpu.make_async_remote_copy(
-                    first.at[unit],
-                    gathered.at[unit, pl.ds(own, 2)],
-                    first_sent.at[unit],
-                    gather_sem.at[unit],
-                    device_id=(section, chip_at(step) * 2 + core),
-                    device_id_type=MESH,
-                ).start()
-            return carry
-
+        for unit in range(LEAD):
+            send_first(unit)
         pltpu.make_async_copy(row_got.at[pl.ds(0, 31)], row_got.at[pl.ds(0, 31)], row_sent).wait()
-        lax.fori_loop(0, UNITS, send_first, 0)
-
-    for load in loads:
-        load.wait()
-    zero_tile = jnp.zeros((BLOCK, BLOCK), jnp.bfloat16)
-    for j in range(HB):
-        down_tiles[j, KMAX] = zero_tile
-    normed[NB] = jnp.zeros((ROWS, BLOCK), jnp.bfloat16)
-
-    def widen(block, carry):
-        columns = pl.ds(pl.multiple_of(block * BLOCK, BLOCK), BLOCK)
-        for side, start in ((0, other_half), (1, half)):
-            for j in range(HB):
-                down_dense[side, pl.ds(j * BLOCK, BLOCK), columns] = down_tiles[j, inverse[j, start + block]]
-        return carry
-
-    lax.fori_loop(0, HALF, widen, 0)
-
-    def work(unit):
+
+    def scale(unit, start):
+        total = jnp.zeros((ROWS, BLOCK), jnp.float32)
+        for b in range(HALF):
+            x = gathered[unit, start + b].astype(jnp.float32)
+            total = total + x * x
+            columns = pl.ds(pl.multiple_of((start + b) * BLOCK, BLOCK), BLOCK)
+            normed[start + b] = (x * gain[0:1, columns]).astype(jnp.bfloat16)
+        return total
+
+    def arrive(unit):
         mine = gathered.at[unit, pl.ds(half, HALF)]
-        theirs = gathered.at[unit, pl.ds(other_half, HALF)]
         pltpu.make_async_copy(mine, mine, gather_sem.at[unit]).wait()
         pltpu.make_async_remote_copy(
             mine, mine, core_sent.at[unit], core_sem.at[unit], device_id=partner, device_id_type=MESH
         ).start()
 
-        squares = jnp.zeros((ROWS, BLOCK), jnp.float32)
-
-        def scale(start, squares):
-            for b in range(HALF):
-                x = gathered[unit, start + b].astype(jnp.float32)
-                squares = squares + x * x
-                columns = pl.ds(pl.multiple_of((start + b) * BLOCK, BLOCK), BLOCK)
-                normed[start + b] = (x * gain[0:1, columns]).astype(jnp.bfloat16)
-            return squares
-
-        squares = scale(half, squares)
+    def multiply(unit):
+        total = scale(unit, half)
+        theirs = gathered.at[unit, pl.ds(other_half, HALF)]
         pltpu.make_async_copy(theirs, theirs, core_sem.at[unit]).wait()
-        squares = scale(other_half, squares)
-        mean = jnp.sum(squares, axis=-1, keepdims=True) * (1.0 / (NB * BLOCK))
+        total = total + scale(unit, other_half)
+        mean = jnp.sum(total, axis=-1, keepdims=True) * (1.0 / (NB * BLOCK))
         row_scale = lax.rsqrt(mean + NORM_EPS)
 
-        hidden = []
+        both = []
         for j in range(HB):
             picked = []
             for k in range(KMAX):
-                slot = in_index[j, k]
+                slot = in_index[0, j, k]
                 picked.append(normed[jnp.where(slot < 0, NB, slot)])
-            both = jnp.dot(
-                jnp.concatenate(picked, axis=1), gate_up[j], preferred_element_type=jnp.float32
+            both.append(
+                jnp.dot(jnp.concatenate(picked, axis=1), gate_up[j], preferred_element_type=jnp.float32)
             )
-            gate_val = both[:, :BLOCK] * row_scale
-            up_val = both[:, BLOCK:] * row_scale
+        hidden = []
+        for j in range(HB):
+            gate_val = both[j][:, :BLOCK] * row_scale
+            up_val = both[j][:, BLOCK:] * row_scale
             hidden.append((gate_val / (1.0 + jnp.exp(-gate_val)) * up_val).astype(jnp.bfloat16))
-        hidden = jnp.concatenate(hidden, axis=1)
-
-        partial = jnp.dot(hidden, down_dense[0], preferred_element_type=jnp.float32)
+
+        for k in range(0, KMAX, 2):
+            for j in range(HB):
+                two = jnp.concatenate([down_tiles[j, k], down_tiles[j, k + 1]], axis=1)
+                product = jnp.dot(hidden[j], two, preferred_element_type=jnp.float32)
+                parts[j, k] = product[:, :BLOCK]
+                parts[j, k + 1] = product[:, BLOCK:]
+
+        def total_of(block):
+            total = parts[0, inverse[0, block]]
+            for j in range(1, HB):
+                total = total + parts[j, inverse[j, block]]
+            return total
+
         for b in range(HALF):
-            given[unit, b] = partial[:, b * BLOCK : (b + 1) * BLOCK].astype(jnp.bfloat16)
+            given[unit, b] = total_of(other_half + b).astype(jnp.bfloat16)
         pltpu.make_async_remote_copy(
             given.at[unit], core_got.at[unit], pair_sent.at[unit], pair_sem.at[unit], device_id=partner, device_id_type=MESH
         ).start()
-        partial = jnp.dot(hidden, down_dense[1], preferred_element_type=jnp.float32)
         for b in range(HALF):
-            kept[b] = partial[:, b * BLOCK : (b + 1) * BLOCK]
+            kept[b] = total_of(half + b)
+
+    def scatter(unit):
         pltpu.make_async_copy(core_got.at[unit], core_got.at[unit], pair_sem.at[unit]).wait()
         for b in range(HALF):
             summed[unit, b] = (kept[b] + core_got[unit, b].astype(jnp.float32)).astype(jnp.bfloat16)
@@ -222,18 +257,30 @@
                     device_id_type=MESH,
                 ).start()
 
-    def turn(unit, carry):
-        @pl.when(unit < UNITS)
-        def _():
-            work(unit)
-
-        @pl.when(unit > 0)
-        def _():
-            finish(unit - 1)
+    def turn(now, carry):
+        @pl.when(now < UNITS)
+        def _():
+            arrive(now)
+
+        @pl.when(now >= LAG)
+        def _():
+            finish(now - LAG)
+
+        @pl.when((section == 0) & (now + LEAD < UNITS))
+        def _():
+            send_first(now + LEAD)
+
+        @pl.when((now >= 1) & (now <= UNITS))
+        def _():
+            scatter(now - 1)
+
+        @pl.when(now < UNITS)
+        def _():
+            multiply(now)
 
         return carry
 
-    lax.fori_loop(0, UNITS + 1, turn, 0)
+    lax.fori_loop(0, UNITS + LAG, turn, 0)
 
     where, block = position(lax.broadcasted_iota(jnp.int32, (512, LIVE), 0))
     at = lax.broadcasted_iota(jnp.int32, (512, LIVE), 1)
@@ -279,23 +326,26 @@
 
 
 def body(tokens, lengths, norm_gain, gate_tiles, up_tiles, in_index, down_tiles, out_index):
-    slots = jnp.arange(KMAX, dtype=jnp.int32)
-    hit = out_index[0][:, None, :] == jnp.arange(NB, dtype=jnp.int32)[None, :, None]
-    inverse = jnp.min(jnp.where(hit, slots, KMAX), axis=-1)
     bf16 = functools.partial(pltpu.VMEM, dtype=jnp.bfloat16)
     dma = pltpu.SemaphoreType.DMA
-    smem = pl.BlockSpec(memory_space=pltpu.SMEM)
     vmem = pl.BlockSpec(memory_space=pltpu.VMEM)
-    hbm = pl.BlockSpec(memory_space=pl.ANY)
+    hbm = pl.BlockSpec(memory_space=pltpu.HBM)
     rows = pl.pallas_call(
         kernel,
         out_shape=jax.ShapeDtypeStruct((8, NB * BLOCK), jnp.bfloat16),
-        in_specs=[smem, smem, smem, vmem, vmem, hbm, hbm, hbm],
+        in_specs=[hbm] * 8,
         out_specs=vmem,
         scratch_shapes=[
+            pltpu.SMEM((4,), jnp.int32),
+            pltpu.SMEM((1, HB, KMAX), jnp.int32),
+            pltpu.SMEM((1, HB, KMAX), jnp.int32),
+            pltpu.SMEM((HB, BLOCK), jnp.int32),
+            pltpu.VMEM((HB, BLOCK), jnp.int32),
+            bf16((4, 2, NB * BLOCK)),
+            pltpu.VMEM((1, NB * BLOCK), jnp.float32),
             bf16((HB, KMAX * BLOCK, 2 * BLOCK)),
-            bf16((HB, KMAX + 1, BLOCK, BLOCK)),
-            bf16((2, HB * BLOCK, HALF * BLOCK)),
+            bf16((HB, KMAX, BLOCK, BLOCK)),
+            pltpu.VMEM((HB, KMAX + 1, ROWS, BLOCK), jnp.float32),
             bf16((UNITS, NB, ROWS, BLOCK)),
             bf16((NB + 1, ROWS, BLOCK)),
             bf16((UNITS, HALF, ROWS, BLOCK)),
@@ -309,6 +359,7 @@
             bf16((32, 16, BLOCK)),
             bf16((32, 16, BLOCK)),
             bf16((32, 16, BLOCK)),
+            dma((6,)),
             dma((3, HB)),
             dma((UNITS,)),
             dma((UNITS,)),
@@ -325,14 +376,14 @@
             dma,
         ],
         compiler_params=pltpu.CompilerParams(
-            collective_id=0, has_side_effects=True, vmem_limit_bytes=52 * 1024 * 1024
+            collective_id=0, has_side_effects=True, vmem_limit_bytes=60 * 1024 * 1024
         ),
         name="relay",
     )(
         lengths,
-        in_index[0],
-        inverse,
-        tokens.reshape(8, NB * BLOCK),
+        in_index,
+        out_index,
+        tokens,
         norm_gain,
         gate_tiles.reshape(HB, KMAX * BLOCK, BLOCK),
         up_tiles.reshape(HB, KMAX * BLOCK, BLOCK),

time: 189 us -> 172 us (0.910)
  Pallas kernels: 184 us -> 170 us
  local copies, waits for them, and re-layouts: 4.58 us -> 1.67 us
    pallas_call x1, Pallas kernels: 184 us -> 170 us  [body(): pl.pallas_call(kernel, out_shape=jax.ShapeDtypeStruct((8, NB * BLOCK), jn...]
    unnamed x6 -> x0, local copies, waits for them, and re-layouts: 2.09 us -> none
where the time goes in v2:
time: 172 us
  Pallas kernels  170 us (99%)
    pallas_call x1, Pallas kernels, body(): pl.pallas_call(kernel, out_shape=jax.ShapeDtypeStruct((8, NB * BLOCK), jn...  170 us

profile of v2, /device:TPU:225, one launch (start us, length us, event | category | flops | bytes accessed | tf_op | source)
XLA Modules:
  0.0 172.0 jit_solution(7592663290013193046)
XLA Ops:
  0.0 170.3 %relay.1 = bf16[8,8192]{1,0:T(8,128)(2,1)} custom-call(s32[4]{0:T(128)} %lengths_in.1, s32[1,4,28]{2,1,0:T(4,128)} %in_index_in.1, s32[1,4,28]{2,1,0:T(4,128)} %out_index_in.1, bf16[4,2,8192]{2,1,0:T(2,128)(2,1)} %tokens_in.1, f32[1,8192]{1,0:T(1,128)} %gain_in.1, bf16[4,3584,128]{2,1,0:T(8,128)(2,1)} %bitcast.3, bf16[4,3584,128]{2,1,0:T(8,128)(2,1)} %bitcast.4, ...), custom_call_target="tpu_custom_call" | custom-call | tf_op jit(solution)/shard_map/relay/pallas_call | solution.py:333
  170.3 1.7 reshape.15

commit v3 on v2

--- a/solution.py
+++ b/solution.py
@@ -18,6 +18,7 @@
 NB = 64
 HALF = NB // 2
 HB = 4
+PIECE = 16
 KMAX = 28
 LAG = 3
 LEAD = 4
@@ -61,8 +62,10 @@
     for load in loads:
         load.start()
 
-    def chip_at(step):
-        return (chip_y + step // SIDE) % SIDE * SIDE + (chip_x + step % SIDE) % SIDE
+    ys = [(chip_y + step) % SIDE * SIDE for step in range(SIDE)]
+    xs = [(chip_x + step) % SIDE for step in range(SIDE)]
+    chips = [y + x for y in ys for x in xs]
+    peers = [there * 2 + core for there in chips]
 
     barrier = pltpu.get_barrier_semaphore()
     before = (section + SECTIONS - 1) % SECTIONS
@@ -134,14 +137,14 @@
         load.wait()
 
     def send_first(unit):
-        pltpu.make_async_copy(first.at[unit], gathered.at[unit, pl.ds(own, 2)], gather_sem.at[unit]).start()
+        pltpu.make_async_copy(first.at[unit], gathered.at[unit, pl.ds(own, 2)], gather_sem.at[unit, chip // 8]).start()
         for step in SEND_ORDER[:-1]:
             pltpu.make_async_remote_copy(
                 first.at[unit],
                 gathered.at[unit, pl.ds(own, 2)],
                 first_sent.at[unit],
-                gather_sem.at[unit],
-                device_id=(section, chip_at(step) * 2 + core),
+                gather_sem.at[unit, chip // 8],
+                device_id=(section, peers[step]),
                 device_id_type=MESH,
             ).start()
 
@@ -161,7 +164,7 @@
 
     def scale(unit, start):
         total = jnp.zeros((ROWS, BLOCK), jnp.float32)
-        for b in range(HALF):
+        for b in range(PIECE):
             x = gathered[unit, start + b].astype(jnp.float32)
             total = total + x * x
             columns = pl.ds(pl.multiple_of((start + b) * BLOCK, BLOCK), BLOCK)
@@ -169,17 +172,19 @@
         return total
 
     def arrive(unit):
-        mine = gathered.at[unit, pl.ds(half, HALF)]
-        pltpu.make_async_copy(mine, mine, gather_sem.at[unit]).wait()
-        pltpu.make_async_remote_copy(
-            mine, mine, core_sent.at[unit], core_sem.at[unit], device_id=partner, device_id_type=MESH
-        ).start()
+        for piece in range(2):
+            mine = gathered.at[unit, pl.ds(half + piece * PIECE, PIECE)]
+            pltpu.make_async_copy(mine, mine, gather_sem.at[unit, piece]).wait()
+            pltpu.make_async_remote_copy(
+                mine, mine, core_sent.at[unit, piece], core_sem.at[unit, piece], device_id=partner, device_id_type=MESH
+            ).start()
 
     def multiply(unit):
-        total = scale(unit, half)
-        theirs = gathered.at[unit, pl.ds(other_half, HALF)]
-        pltpu.make_async_copy(theirs, theirs, core_sem.at[unit]).wait()
-        total = total + scale(unit, other_half)
+        total = scale(unit, half) + scale(unit, half + PIECE)
+        for piece in range(2):
+            theirs = gathered.at[unit, pl.ds(other_half + piece * PIECE, PIECE)]
+            pltpu.make_async_copy(theirs, theirs, core_sem.at[unit, piece]).wait()
+            total = total + scale(unit, other_half + piece * PIECE)
         mean = jnp.sum(total, axis=-1, keepdims=True) * (1.0 / (NB * BLOCK))
         row_scale = lax.rsqrt(mean + NORM_EPS)
 
@@ -224,13 +229,13 @@
         for b in range(HALF):
             summed[unit, b] = (kept[b] + core_got[unit, b].astype(jnp.float32)).astype(jnp.bfloat16)
         for step in SEND_ORDER[:-1]:
-            there = chip_at(step)
+            there = chips[step]
             pltpu.make_async_remote_copy(
                 summed.at[unit, pl.ds(there * 2, 2)],
                 got.at[unit, chip],
                 scatter_sent.at[unit],
                 scatter_sem.at[unit],
-                device_id=(section, there * 2 + core),
+                device_id=(section, peers[step]),
                 device_id_type=MESH,
             ).start()
         pltpu.make_async_copy(
@@ -252,8 +257,8 @@
                     result.at[unit],
                     gathered.at[unit, pl.ds(own, 2)],
                     gather_sent.at[unit],
-                    gather_sem.at[unit],
-                    device_id=(section + 1, chip_at(step) * 2 + core),
+                    gather_sem.at[unit, chip // 8],
+                    device_id=(section + 1, peers[step]),
                     device_id_type=MESH,
                 ).start()
 
@@ -301,9 +306,10 @@
     lax.fori_loop(1, 32, send_out, 0)
 
     def drain(unit, carry):
-        mine = gathered.at[unit, pl.ds(half, HALF)]
         sent = got.at[unit, pl.ds(0, CHIPS - 1)]
-        pltpu.make_async_copy(mine, mine, core_sent.at[unit]).wait()
+        for piece in range(2):
+            mine = gathered.at[unit, pl.ds(half + piece * PIECE, PIECE)]
+            pltpu.make_async_copy(mine, mine, core_sent.at[unit, piece]).wait()
         pltpu.make_async_copy(given.at[unit], given.at[unit], pair_sent.at[unit]).wait()
         pltpu.make_async_copy(sent, sent, scatter_sent.at[unit]).wait()
 
@@ -361,10 +367,10 @@
             bf16((32, 16, BLOCK)),
             dma((6,)),
             dma((3, HB)),
-            dma((UNITS,)),
-            dma((UNITS,)),
-            dma((UNITS,)),
-            dma((UNITS,)),
+            dma((UNITS, 2)),
+            dma((UNITS,)),
+            dma((UNITS, 2)),
+            dma((UNITS, 2)),
             dma((UNITS,)),
             dma((UNITS,)),
             dma((UNITS,)),

time: 172 us -> 171 us (level)
  no operation moved by 1% of the time
where the time goes in v3:
time: 171 us
  Pallas kernels  169 us (99%)
    pallas_call x1, Pallas kernels, body(): pl.pallas_call(kernel, out_shape=jax.ShapeDtypeStruct((8, NB * BLOCK), jn...  169 us

profile of v3, /device:TPU:225, one launch (start us, length us, event | category | flops | bytes accessed | tf_op | source)
XLA Modules:
  0.0 171.0 jit_solution(9156251156393810170)
XLA Ops:
  0.0 169.3 %relay.1 = bf16[8,8192]{1,0:T(8,128)(2,1)} custom-call(s32[4]{0:T(128)} %lengths_in.1, s32[1,4,28]{2,1,0:T(4,128)} %in_index_in.1, s32[1,4,28]{2,1,0:T(4,128)} %out_index_in.1, bf16[4,2,8192]{2,1,0:T(2,128)(2,1)} %tokens_in.1, f32[1,8192]{1,0:T(1,128)} %gain_in.1, bf16[4,3584,128]{2,1,0:T(8,128)(2,1)} %bitcast.3, bf16[4,3584,128]{2,1,0:T(8,128)(2,1)} %bitcast.4, ...), custom_call_target="tpu_custom_call" | custom-call | tf_op jit(solution)/shard_map/relay/pallas_call | solution.py:339
  169.4 1.7 reshape.15

commit v4 on v2

--- a/solution.py
+++ b/solution.py
@@ -18,9 +18,10 @@
 NB = 64
 HALF = NB // 2
 HB = 4
+PIECE = 16
 KMAX = 28
 LAG = 3
-LEAD = 4
+LEAD = 3
 MESH = pl.DeviceIdType.MESH
 SEND_ORDER = sorted(range(CHIPS), key=lambda step: -sum(min(d, SIDE - d) for d in divmod(step, SIDE)))
 
@@ -28,7 +29,7 @@
 def kernel(
     lengths_in, in_index_in, out_index_in, tokens_in, gain_in, gate, up, down, out,
     lengths, in_index, out_index, inverse, inverse_rows, tokens, gain,
-    gate_up, down_tiles, parts, gathered, normed, given, kept, core_got, summed, got, first, result,
+    gate_up, down_tiles, parts, gathered, normed, given, kept, core_got, summed, got, first, result, places,
     row_send, row_got, out_send, out_got,
     small_sem, load_sem, gather_sem, gather_sent, core_sem, core_sent, pair_sem, pair_sent,
     scatter_sem, scatter_sent, first_sent, row_sem, row_sent, out_sem, out_sent,
@@ -43,6 +44,22 @@
     other_half = HALF - half
     own = half + chip * 2
     partner = (section, chip * 2 + 1 - core)
+
+    ys = [(chip_y + step) % SIDE * SIDE for step in range(SIDE)]
+    xs = [(chip_x + step) % SIDE for step in range(SIDE)]
+    chips = [y + x for y in ys for x in xs]
+    peers = [there * 2 + core for there in chips]
+
+    barrier = pltpu.get_barrier_semaphore()
+    before = (section + SECTIONS - 1) % SECTIONS
+    others = []
+    for step in SEND_ORDER:
+        pl.semaphore_signal(barrier, inc=1, device_id=(before, peers[step]), device_id_type=MESH)
+        others.append(chips[step] * 2 + 1 - core)
+        if step > 0:
+            others.append(peers[step])
+    for there in others:
+        pl.semaphore_signal(barrier, inc=1, device_id=(section, there), device_id_type=MESH)
 
     smalls = [
         pltpu.make_async_copy(lengths_in, lengths, small_sem.at[0]),
@@ -61,23 +78,6 @@
     for load in loads:
         load.start()
 
-    def chip_at(step):
-        return (chip_y + step // SIDE) % SIDE * SIDE + (chip_x + step % SIDE) % SIDE
-
-    barrier = pltpu.get_barrier_semaphore()
-    before = (section + SECTIONS - 1) % SECTIONS
-
-    def greet_plane(step, carry):
-        pl.semaphore_signal(barrier, inc=1, device_id=(section, (shard + step) % 32), device_id_type=MESH)
-        return carry
-
-    def greet_before(step, carry):
-        pl.semaphore_signal(barrier, inc=1, device_id=(before, step * 2 + core), device_id_type=MESH)
-        return carry
-
-    lax.fori_loop(1, 32, greet_plane, 0)
-    lax.fori_loop(0, CHIPS, greet_before, 0)
-
     for small in smalls:
         small.wait()
     offsets = [jnp.int32(0)]
@@ -114,6 +114,11 @@
             rows = [tokens[m, :, pl.ds(b * BLOCK, BLOCK)].astype(jnp.float32) for m in range(4)]
             row_send[owner, pl.ds(b % 2 * 8, 8), :] = jnp.concatenate(rows, axis=0).astype(jnp.bfloat16)
 
+    where, block = position(lax.broadcasted_iota(jnp.int32, (512, LIVE), 0))
+    at = lax.broadcasted_iota(jnp.int32, (512, LIVE), 1)
+    for b in range(2):
+        places[b] = jnp.where((where == at) & (block == b), 1.0, 0.0).astype(jnp.bfloat16)
+
     inverse_copy.wait()
     pl.semaphore_wait(barrier, 31 + CHIPS)
 
@@ -121,14 +126,10 @@
     def _():
         pltpu.make_async_copy(row_send.at[shard], row_got.at[shard], row_sem).start()
 
-        def send_rows(step, carry):
-            there = (shard + step) % 32
+        for there in others:
             pltpu.make_async_remote_copy(
                 row_send.at[there], row_got.at[shard], row_sent, row_sem, device_id=(section, there), device_id_type=MESH
             ).start()
-            return carry
-
-        lax.fori_loop(1, 32, send_rows, 0)
 
     for load in loads:
         load.wait()
@@ -141,7 +142,7 @@
                 gathered.at[unit, pl.ds(own, 2)],
                 first_sent.at[unit],
                 gather_sem.at[unit],
-                device_id=(section, chip_at(step) * 2 + core),
+                device_id=(section, peers[step]),
                 device_id_type=MESH,
             ).start()
 
@@ -211,31 +212,41 @@
                 total = total + parts[j, inverse[j, block]]
             return total
 
-        for b in range(HALF):
-            given[unit, b] = total_of(other_half + b).astype(jnp.bfloat16)
-        pltpu.make_async_remote_copy(
-            given.at[unit], core_got.at[unit], pair_sent.at[unit], pair_sem.at[unit], device_id=partner, device_id_type=MESH
-        ).start()
-        for b in range(HALF):
-            kept[b] = total_of(half + b)
-
-    def scatter(unit):
-        pltpu.make_async_copy(core_got.at[unit], core_got.at[unit], pair_sem.at[unit]).wait()
-        for b in range(HALF):
-            summed[unit, b] = (kept[b] + core_got[unit, b].astype(jnp.float32)).astype(jnp.bfloat16)
-        for step in SEND_ORDER[:-1]:
-            there = chip_at(step)
+        for piece in range(2):
+            for at in range(piece * PIECE, (piece + 1) * PIECE):
+                block = chips[SEND_ORDER[at // 2]] * 2 + at % 2
+                given[unit, at] = total_of(other_half + block).astype(jnp.bfloat16)
+            part = pl.ds(piece * PIECE, PIECE)
             pltpu.make_async_remote_copy(
-                summed.at[unit, pl.ds(there * 2, 2)],
-                got.at[unit, chip],
-                scatter_sent.at[unit],
-                scatter_sem.at[unit],
-                device_id=(section, there * 2 + core),
+                given.at[unit, part],
+                core_got.at[unit, part],
+                pair_sent.at[unit, piece],
+                pair_sem.at[unit, piece],
+                device_id=partner,
                 device_id_type=MESH,
             ).start()
-        pltpu.make_async_copy(
-            summed.at[unit, pl.ds(chip * 2, 2)], got.at[unit, chip], scatter_sem.at[unit]
-        ).start()
+        for at in range(HALF):
+            kept[at] = total_of(half + chips[SEND_ORDER[at // 2]] * 2 + at % 2)
+
+    def scatter(unit):
+        for piece in range(2):
+            part = core_got.at[unit, pl.ds(piece * PIECE, PIECE)]
+            pltpu.make_async_copy(part, part, pair_sem.at[unit, piece]).wait()
+            for at in range(piece * PIECE, (piece + 1) * PIECE):
+                summed[unit, at] = (kept[at] + core_got[unit, at].astype(jnp.float32)).astype(jnp.bfloat16)
+            for at in range(piece * PIECE // 2, (piece + 1) * PIECE // 2):
+                ours = summed.at[unit, pl.ds(at * 2, 2)]
+                if at == CHIPS - 1:
+                    pltpu.make_async_copy(ours, got.at[unit, chip], scatter_sem.at[unit]).start()
+                else:
+                    pltpu.make_async_remote_copy(
+                        ours,
+                        got.at[unit, chip],
+                        scatter_sent.at[unit],
+                        scatter_sem.at[unit],
+                        device_id=(section, peers[SEND_ORDER[at]]),
+                        device_id_type=MESH,
+                    ).start()
 
     def finish(unit):
         pltpu.make_async_copy(got.at[unit], got.at[unit], scatter_sem.at[unit]).wait()
@@ -253,7 +264,7 @@
                     gathered.at[unit, pl.ds(own, 2)],
                     gather_sent.at[unit],
                     gather_sem.at[unit],
-                    device_id=(section + 1, chip_at(step) * 2 + core),
+                    device_id=(section + 1, peers[step]),
                     device_id_type=MESH,
                 ).start()
 
@@ -282,29 +293,24 @@
 
     lax.fori_loop(0, UNITS + LAG, turn, 0)
 
-    where, block = position(lax.broadcasted_iota(jnp.int32, (512, LIVE), 0))
-    at = lax.broadcasted_iota(jnp.int32, (512, LIVE), 1)
     spread = jnp.zeros((512, BLOCK), jnp.float32)
     for b in range(2):
-        place = jnp.where((where == at) & (block == b), 1.0, 0.0).astype(jnp.bfloat16)
-        spread = spread + jnp.dot(place, result[:, b].reshape(LIVE, BLOCK), preferred_element_type=jnp.float32)
+        spread = spread + jnp.dot(places[b], result[:, b].reshape(LIVE, BLOCK), preferred_element_type=jnp.float32)
     out_send[...] = spread.astype(jnp.bfloat16).reshape(32, 16, BLOCK)
     pltpu.make_async_copy(out_send.at[shard], out_got.at[shard], out_sem).start()
 
-    def send_out(step, carry):
-        there = (shard + step) % 32
+    for there in others:
         pltpu.make_async_remote_copy(
             out_send.at[there], out_got.at[shard], out_sent, out_sem, device_id=(section, there), device_id_type=MESH
         ).start()
-        return carry
-
-    lax.fori_loop(1, 32, send_out, 0)
 
     def drain(unit, carry):
         mine = gathered.at[unit, pl.ds(half, HALF)]
         sent = got.at[unit, pl.ds(0, CHIPS - 1)]
         pltpu.make_async_copy(mine, mine, core_sent.at[unit]).wait()
-        pltpu.make_async_copy(given.at[unit], given.at[unit], pair_sent.at[unit]).wait()
+        for piece in range(2):
+            part = given.at[unit, pl.ds(piece * PIECE, PIECE)]
+            pltpu.make_async_copy(part, part, pair_sent.at[unit, piece]).wait()
         pltpu.make_async_copy(sent, sent, scatter_sent.at[unit]).wait()
 
         @pl.when(section < SECTIONS - 1)
@@ -355,6 +361,7 @@
             bf16((UNITS, CHIPS, 2, ROWS, BLOCK)),
             bf16((UNITS, 2, ROWS, BLOCK)),
             bf16((UNITS, 2, ROWS, BLOCK)),
+            bf16((2, 512, LIVE)),
             bf16((32, 16, BLOCK)),
             bf16((32, 16, BLOCK)),
             bf16((32, 16, BLOCK)),
@@ -365,8 +372,8 @@
             dma((UNITS,)),
             dma((UNITS,)),
             dma((UNITS,)),
-            dma((UNITS,)),
-            dma((UNITS,)),
+            dma((UNITS, 2)),
+            dma((UNITS, 2)),
             dma((UNITS,)),
             dma((UNITS,)),
             dma((UNITS,)),

time: 172 us -> 172 us (level)
  no operation moved by 1% of the time
where the time goes in v4:
time: 172 us
  Pallas kernels  170 us (99%)
    pallas_call x1, Pallas kernels, body(): pl.pallas_call(kernel, out_shape=jax.ShapeDtypeStruct((8, NB * BLOCK), jn...  170 us

profile of v4, /device:TPU:225, one launch (start us, length us, event | category | flops | bytes accessed | tf_op | source)
XLA Modules:
  0.0 172.1 jit_solution(2319479702841853710)
XLA Ops:
  0.0 170.4 %relay.1 = bf16[8,8192]{1,0:T(8,128)(2,1)} custom-call(s32[4]{0:T(128)} %lengths_in.1, s32[1,4,28]{2,1,0:T(4,128)} %in_index_in.1, s32[1,4,28]{2,1,0:T(4,128)} %out_index_in.1, bf16[4,2,8192]{2,1,0:T(2,128)(2,1)} %tokens_in.1, f32[1,8192]{1,0:T(1,128)} %gain_in.1, bf16[4,3584,128]{2,1,0:T(8,128)(2,1)} %bitcast.3, bf16[4,3584,128]{2,1,0:T(8,128)(2,1)} %bitcast.4, ...), custom_call_target="tpu_custom_call" | custom-call | tf_op jit(solution)/shard_map/relay/pallas_call | solution.py:339
  170.4 1.7 reshape.15
